TPU v7x, 32 devices: a whole 2x2x4 slice. The times are simulated.
32 devices in a mesh: seq: 8 (over y, x, core), grp: 4 (over z).
Axes of the slice: x: 2, y: 2, z: 4, core: 2. Of those that a mesh axis runs over, the one named last changes fastest.
Arguments:
- normed_hidden_input: bfloat16 [4096, 4096], P(('grp', 'seq')), may hold values from -6 to 6
- frozen_query_rows: bfloat16 [4096, 4096], P(('grp', 'seq')), may hold values from -16 to 16
- frozen_key_rows: bfloat16 [4096, 1024], P(('grp', 'seq')), may hold values from -16 to 16
- attention_output_gradient: bfloat16 [4096, 4096], P(('grp', 'seq')), may hold values from -0.15625 to 0.15625
- adapter_down_weight: bfloat16 [64, 64, 4096], P('grp', None, 'seq'), may hold values from -0.09375 to 0.09375
- adapter_up_weight: bfloat16 [64, 64, 1024], P('grp', 'seq'), may hold values from -0.75 to 0.75
- segment_adapter_index: int32 [4, 4], replicated, may hold values from 0 to 63, as said below
- segment_block_count: int32 [4, 4], replicated, may hold values from 1 to 4, 8 in all within a row
- adapter_row_index: int32 [64], replicated, may hold values from 0 to 63, as said below
Outputs:
- down_grad: float32 [64, 64, 4096], P('grp', None, 'seq')
- up_grad: float32 [64, 64, 1024], P('grp', 'seq')
Inputs may be any that keep to these rules, and one draw needn't show every extreme that they name: A permutation: adapter a is held in row adapter_row_index[a] of adapter_down_weight and adapter_up_weight. `segment_adapter_index`: call rows g * 16 to (g + 1) * 16 - 1 of adapter_down_weight the rows of index g of grp. In each sequence at most 2 segments use adapters held in the rows of one index of grp, and in every sequence some index holds exactly 2 of them. Tenants may repeat within and across sequences. `segment_block_count`: each row sums to 8; in each row some segment has exactly 4 blocks.
All inputs are finite; a program needn't handle non-finite values.
Results may differ from a plain program's by a relative error of at most 0.0056.
Values may be sent and summed in bfloat16 or wider, within the bound.
A program may use at most 64 MiB of HBM per device.

v0:
```python
import math

import jax
import jax.numpy as jnp
from jax import lax
from jax.sharding import PartitionSpec as P

HEAD_DIM = 128
BLOCK = 128
QROWS = 512


adapter_scale = 2.0


def attend_head(query_head, key_head, grad_head, segment_ids, query_rows, reach):
    length, head_width = query_head.shape
    padded_keys = jnp.concatenate([jnp.zeros((reach, head_width), key_head.dtype), key_head], 0)
    padded_ids = jnp.concatenate([jnp.full((reach,), -1, jnp.int32), segment_ids], 0)
    window = query_rows + reach
    factor = 1.0 / math.sqrt(head_width)

    def one_block(totals, number):
        offset = number * query_rows
        query_block = lax.dynamic_slice_in_dim(query_head, offset, query_rows, 0)
        grad_block = lax.dynamic_slice_in_dim(grad_head, offset, query_rows, 0)
        key_block = lax.dynamic_slice_in_dim(padded_keys, offset, window, 0)
        key_ids = lax.dynamic_slice_in_dim(padded_ids, offset, window, 0)
        query_ids = lax.dynamic_slice_in_dim(segment_ids, offset, query_rows, 0)
        scores = jnp.dot(query_block, key_block.T, preferred_element_type=jnp.float32) * factor
        query_pos = offset + jnp.arange(query_rows, dtype=jnp.int32)
        key_pos = offset - reach + jnp.arange(window, dtype=jnp.int32)
        allowed = (key_ids[None, :] == query_ids[:, None]) & (
            key_pos[None, :] <= query_pos[:, None]
        )
        scores = jnp.where(allowed, scores, jnp.float32(-1e30))
        highest = jnp.max(scores, axis=1, keepdims=True)
        expo = jnp.exp(scores - highest)
        probabilities = (expo / jnp.sum(expo, axis=1, keepdims=True)).astype(jnp.bfloat16)
        contribution = jnp.dot(probabilities.T, grad_block, preferred_element_type=jnp.float32)
        current = lax.dynamic_slice_in_dim(totals, offset, window, 0)
        totals = lax.dynamic_update_slice_in_dim(totals, current + contribution, offset, 0)
        return (totals, None)

    initial = jnp.zeros((length + reach, head_width), jnp.float32)
    totals, _ = lax.scan(one_block, initial, jnp.arange(length // query_rows, dtype=jnp.int32))
    return totals[reach:].astype(jnp.bfloat16)


def local(
    normed_hidden_input,
    frozen_query_rows,
    frozen_key_rows,
    attention_output_gradient,
    adapter_down_weight,
    adapter_up_weight,
    segment_adapter_index,
    segment_block_count,
    adapter_row_index,
):
    group_count = lax.axis_size("grp")
    shard_count = lax.axis_size("seq")
    group_index = lax.axis_index("grp")
    tokens_here, model_width = normed_hidden_input.shape
    portion_width = adapter_down_weight.shape[2]
    resident_adapters, rank_overall = (adapter_down_weight.shape[0], adapter_down_weight.shape[1])
    rank_portion, value_projection_width = (adapter_up_weight.shape[1], adapter_up_weight.shape[2])
    segments = segment_adapter_index.shape[1]
    capacity = max(2, (segments + group_count - 1) // group_count)
    seq_length = tokens_here * shard_count
    block_total = seq_length // BLOCK
    block_here = tokens_here // BLOCK
    reach = min(16, seq_length // (2 * BLOCK)) * BLOCK
    head_total = frozen_query_rows.shape[1] // HEAD_DIM
    kv_heads = value_projection_width // HEAD_DIM
    heads_here = head_total // shard_count
    group_size = head_total // kv_heads
    slot_total = group_count * capacity
    adapter_ids = jnp.arange(adapter_row_index.shape[0], dtype=jnp.int32)
    slot_of = jnp.sum(
        jnp.where(segment_adapter_index[:, :, None] == adapter_ids, adapter_row_index, 0), axis=2
    )
    owner_group = slot_of // resident_adapters
    local_slot = slot_of % resident_adapters
    order_ids = jnp.arange(segments, dtype=jnp.int32)
    earlier = order_ids[:, None] > order_ids[None, :]
    same_owner = owner_group[:, :, None] == owner_group[:, None, :]
    rank_in_owner = jnp.sum((same_owner & earlier[None]).astype(jnp.int32), axis=2)
    placement = owner_group * capacity + rank_in_owner
    capacity_ids = jnp.arange(capacity, dtype=jnp.int32)
    local_ids = jnp.arange(resident_adapters, dtype=jnp.int32)
    picks = (
        (owner_group == group_index)[:, :, None, None]
        & (rank_in_owner[:, :, None, None] == capacity_ids[:, None])
        & (local_slot[:, :, None, None] == local_ids)
    )
    chooser = jnp.sum(picks.astype(jnp.float32), axis=1)
    selector_half = chooser.astype(jnp.bfloat16)
    send_down = jnp.einsum(
        "pgl,lut->pgut", selector_half, adapter_down_weight, preferred_element_type=jnp.float32
    ).astype(jnp.bfloat16)
    send_up = jnp.einsum(
        "gyv,vmf->gymf", selector_half, adapter_up_weight, preferred_element_type=jnp.float32
    ).astype(jnp.bfloat16)
    fetched_down, fetched_up = (
        lax.all_to_all(send_down, "grp", split_axis=0, concat_axis=0, tiled=True),
        lax.all_to_all(send_up, "grp", split_axis=0, concat_axis=0, tiled=True),
    )
    own_blocks = segment_block_count[group_index]
    ends = jnp.cumsum(own_blocks)
    block_seg = jnp.sum(
        (jnp.arange(block_total, dtype=jnp.int32)[:, None] >= ends[None, :]).astype(jnp.int32),
        axis=1,
    )
    own_place = placement[group_index]
    block_place = jnp.sum(
        jnp.where(block_seg[:, None] == order_ids[None, :], own_place[None, :], 0), axis=1
    )
    block_pick = block_place[:, None] == jnp.arange(slot_total, dtype=jnp.int32)[None, :]
    pick_half = block_pick.astype(jnp.bfloat16)
    segment_ids = jnp.broadcast_to(block_seg[:, None], (block_total, BLOCK)).reshape(seq_length)
    block_down_weight = jnp.einsum(
        "bn,nrd->brd",
        pick_half,
        fetched_down.reshape(slot_total, rank_overall, portion_width),
        preferred_element_type=jnp.float32,
    ).astype(jnp.bfloat16)
    block_up_rows = jnp.einsum(
        "bn,nre->bre",
        pick_half,
        fetched_up.reshape(slot_total, rank_portion, value_projection_width),
        preferred_element_type=jnp.float32,
    ).astype(jnp.bfloat16)
    features = lax.all_to_all(normed_hidden_input, "seq", split_axis=1, concat_axis=0, tiled=True)
    amount = lax.axis_size("seq") * tokens_here
    token_rows = features.reshape(amount // BLOCK, BLOCK, portion_width)
    reduced_rank_part = (
        lax.psum_scatter(
            jnp.einsum(
                "jyw,jaw->jya", token_rows, block_down_weight, preferred_element_type=jnp.float32
            ).reshape(amount, rank_overall),
            "seq",
            scatter_dimension=0,
            tiled=True,
        )
        .astype(jnp.bfloat16)
        .reshape(block_here, BLOCK, rank_overall)
    )
    near_up = lax.all_to_all(block_up_rows, "seq", split_axis=0, concat_axis=1, tiled=True)
    query_grid = frozen_query_rows.reshape(tokens_here, shard_count, heads_here, HEAD_DIM)
    key_grid = jnp.repeat(
        frozen_key_rows.reshape(tokens_here, kv_heads, HEAD_DIM), group_size, axis=1
    ).reshape(tokens_here, shard_count, heads_here, HEAD_DIM)
    grad_grid = attention_output_gradient.reshape(tokens_here, shard_count, heads_here, HEAD_DIM)
    query_all = lax.all_to_all(query_grid, "seq", split_axis=1, concat_axis=0, tiled=True)
    key_all = lax.all_to_all(key_grid, "seq", split_axis=1, concat_axis=0, tiled=True)
    grad_all = lax.all_to_all(grad_grid, "seq", split_axis=1, concat_axis=0, tiled=True)

    def per_head(triple):
        return attend_head(triple[0], triple[1], triple[2], segment_ids, QROWS, reach)

    stacked = (
        jnp.moveaxis(query_all[:, 0], 1, 0),
        jnp.moveaxis(key_all[:, 0], 1, 0),
        jnp.moveaxis(grad_all[:, 0], 1, 0),
    )
    result = lax.map(per_head, stacked)
    head_grads = jnp.moveaxis(result, 0, 1)[:, None]
    token_grads = lax.all_to_all(head_grads, "seq", split_axis=0, concat_axis=1, tiled=True)
    value_grad = jnp.sum(
        token_grads.reshape(tokens_here, kv_heads, group_size, HEAD_DIM), axis=2, dtype=jnp.float32
    )
    value_row_blocks = value_grad.reshape(block_here, BLOCK, value_projection_width).astype(
        jnp.bfloat16
    )
    up_weight_terms = adapter_scale * jnp.einsum(
        "fvg,fvn->fgn", reduced_rank_part, value_row_blocks, preferred_element_type=jnp.float32
    )
    backward_rank_part = (
        adapter_scale
        * jnp.einsum("vaw,vpw->vap", value_row_blocks, near_up, preferred_element_type=jnp.float32)
    ).astype(jnp.bfloat16)
    all_low = lax.all_gather(
        backward_rank_part.reshape(tokens_here, rank_overall), "seq", axis=0, tiled=True
    )
    back_down = jnp.einsum(
        "jcy,jct->jyt",
        all_low.reshape(block_total, BLOCK, rank_overall),
        features.reshape(block_total, BLOCK, portion_width),
        preferred_element_type=jnp.float32,
    )
    back_up = lax.all_to_all(up_weight_terms, "seq", split_axis=1, concat_axis=0, tiled=True)
    pick_full = block_pick.astype(jnp.float32)
    slot_down = jnp.einsum("bn,brd->nrd", pick_full, back_down, precision=lax.Precision.HIGHEST)
    slot_up = jnp.einsum("bn,bre->nre", pick_full, back_up, precision=lax.Precision.HIGHEST)
    return_down, return_up = (
        lax.all_to_all(
            slot_down.reshape(group_count, capacity, rank_overall, portion_width),
            "grp",
            split_axis=0,
            concat_axis=0,
            tiled=True,
        ),
        lax.all_to_all(
            slot_up.reshape(group_count, capacity, rank_portion, value_projection_width),
            "grp",
            split_axis=0,
            concat_axis=0,
            tiled=True,
        ),
    )
    down_grad = jnp.einsum("nca,ncrd->ard", chooser, return_down, precision=lax.Precision.HIGHEST)
    up_grad = jnp.einsum("nca,ncre->are", chooser, return_up, precision=lax.Precision.HIGHEST)
    return (down_grad, up_grad)


def solution(mesh):
    return jax.shard_map(
        local,
        mesh=mesh,
        in_specs=(
            P(("grp", "seq"), None),
            P(("grp", "seq"), None),
            P(("grp", "seq"), None),
            P(("grp", "seq"), None),
            P("grp", None, "seq"),
            P("grp", "seq", None),
            P(),
            P(),
            P(),
        ),
        out_specs=(P("grp", None, "seq"), P("grp", "seq", None)),
        check_vma=False,
    )
```

profile of v0, /device:TPU:0, one launch (start us, length us, event | category | flops | bytes accessed | tf_op | source)
XLA Modules:
  0.0 257.7 jit_solution(14914157780217661762)
XLA Ops:
  10.5 6.3 %all-to-all-start.4 = ((bf16[4,2,8,1024]{3,2,1,0:T(8,128)(2,1)}), bf16[4,2,8,1024]{3,2,1,0:T(8,128)(2,1)S(1)}, u32[]{:S(2)}, u32[]{:S(2)}) async-start(bf16[4,2,8,1024]{3,2,1,0:T(8,128)(2,1)} %copy.126), calls=%async_computation.4 | async-start | bytes 262144 | tf_op jit(solution)/shard_map/all_to_all | solution.py:107
  19.8 3.1 %all-to-all-done.4 = bf16[4,2,8,1024]{3,2,1,0:T(8,128)(2,1)S(1)} async-done(((bf16[4,2,8,1024]{3,2,1,0:T(8,128)(2,1)}), bf16[4,2,8,1024]{3,2,1,0:T(8,128)(2,1)S(1)}, u32[]{:S(2)}, u32[]{:S(2)}) %all-to-all-start.4) | async-done | bytes 131104 | tf_op jit(solution)/shard_map/all_to_all | solution.py:107
  22.9 3.7 %all-to-all-start = ((bf16[128,8,4,128]{3,0,2,1:T(8,128)(2,1)}), bf16[128,8,4,128]{3,0,2,1:T(8,128)(2,1)S(1)}, u32[]{:S(2)}, u32[]{:S(2)}) async-start(bf16[128,8,4,128]{3,0,2,1:T(8,128)(2,1)} %copy.115), calls=%async_computation | async-start | bytes 2097152 | tf_op jit(solution)/shard_map/all_to_all | solution.py:155
  28.6 13.4 %all-to-all-done = bf16[128,8,4,128]{3,0,2,1:T(8,128)(2,1)S(1)} async-done(((bf16[128,8,4,128]{3,0,2,1:T(8,128)(2,1)}), bf16[128,8,4,128]{3,0,2,1:T(8,128)(2,1)S(1)}, u32[]{:S(2)}, u32[]{:S(2)}) %all-to-all-start) | async-done | bytes 1048608 | tf_op jit(solution)/shard_map/all_to_all | solution.py:155
  42.0 3.6 %all-to-all-start.1 = ((bf16[128,8,4,128]{3,0,2,1:T(8,128)(2,1)}), bf16[128,8,4,128]{3,0,2,1:T(8,128)(2,1)S(1)}, u32[]{:S(2)}, u32[]{:S(2)}) async-start(bf16[128,8,4,128]{3,0,2,1:T(8,128)(2,1)} %copy.118), calls=%async_computation.1 | async-start | bytes 2097152 | tf_op jit(solution)/shard_map/all_to_all | solution.py:157
  45.7 15.3 %all-to-all-done.1 = bf16[128,8,4,128]{3,0,2,1:T(8,128)(2,1)S(1)} async-done(((bf16[128,8,4,128]{3,0,2,1:T(8,128)(2,1)}), bf16[128,8,4,128]{3,0,2,1:T(8,128)(2,1)S(1)}, u32[]{:S(2)}, u32[]{:S(2)}) %all-to-all-start.1) | async-done | bytes 1048608 | tf_op jit(solution)/shard_map/all_to_all | solution.py:157
  62.2 3.6 %all-to-all-start.2 = ((bf16[128,8,4,128]{3,0,2,1:T(8,128)(2,1)}), bf16[128,8,4,128]{3,0,2,1:T(8,128)(2,1)S(1)}, u32[]{:S(2)}, u32[]{:S(2)}) async-start(bf16[128,8,4,128]{3,0,2,1:T(8,128)(2,1)} %broadcast_in_dim.80), calls=%async_computation.2 | async-start | bytes 2097152 | tf_op jit(solution)/shard_map/all_to_all | solution.py:156
  65.7 1.9 convolution_convert_fusion.1
  68.5 12.5 %all-to-all-done.2 = bf16[128,8,4,128]{3,0,2,1:T(8,128)(2,1)S(1)} async-done(((bf16[128,8,4,128]{3,0,2,1:T(8,128)(2,1)}), bf16[128,8,4,128]{3,0,2,1:T(8,128)(2,1)S(1)}, u32[]{:S(2)}, u32[]{:S(2)}) %all-to-all-start.2) | async-done | bytes 1048608 | tf_op jit(solution)/shard_map/all_to_all | solution.py:156
  81.1 4.1 %all-to-all-start.8 = ((bf16[4,2,64,512]{3,2,1,0:T(8,128)(2,1)}), bf16[4,2,64,512]{3,2,1,0:T(8,128)(2,1)}, u32[]{:S(2)}, u32[]{:S(2)}) async-start(bf16[4,2,64,512]{3,2,1,0:T(8,128)(2,1)} %copy.139), calls=%async_computation.8 | async-start | bytes 1048576 | tf_op jit(solution)/shard_map/all_to_all | solution.py:106
  86.6 2.3 copy.129
  88.9 2.3 copy.130
  95.2 1.9 all-to-all-done.8
  97.2 4.9 %all-to-all-start.6 = ((bf16[128,8,512]{2,0,1:T(8,128)(2,1)}), bf16[128,8,512]{2,0,1:T(8,128)(2,1)S(1)}, u32[]{:S(2)}, u32[]{:S(2)}) async-start(bf16[128,8,512]{2,0,1:T(8,128)(2,1)} %copy.130), calls=%async_computation.6 | async-start | bytes 2097152 | tf_op jit(solution)/shard_map/all_to_all | solution.py:134
  102.0 40.3 %while.34 = (s32[]{:T(128)}, bf16[4,1024,128]{2,1,0:T(8,128)(2,1)}, bf16[4,1024,128]{2,1,0:T(8,128)(2,1)}, bf16[4,1024,128]{2,1,0:T(8,128)(2,1)}, bf16[4,1024,12...) while((s32[]{:T(128)}, bf16[4,1024,128]{2,1,0:T(8,128)(2,1)}, ...), condition=%wide.region_11.12_spmd.clone, body=%wide.region_6.11_spmd.clone.sunk | while | flops 274334208 | bytes 11459667 | solution.py:167
  104.3 7.1 %while.35 = (s32[]{:T(128)}, f32[1536,128]{1,0:T(8,128)S(1)}, s32[2]{0:T(128)S(1)}, s32[1536]{0:T(1024)S(1)}, s32[1024]{0:T(1024)S(1)}, /*index=5*/bf16[1024,128...) while((s32[]{:T(128)}, f32[1536,128]{1,0:T(8,128)S(1)}, ...), condition=%wide.region_10.10_spmd, body=%wide.region_7.9_spmd.sunk | while | flops 274334208 | bytes 7905540 | solution.py:46
  114.3 7.1 %while.35 = (s32[]{:T(128)}, f32[1536,128]{1,0:T(8,128)S(1)}, s32[2]{0:T(128)S(1)}, s32[1536]{0:T(1024)S(1)}, s32[1024]{0:T(1024)S(1)}, /*index=5*/bf16[1024,128...) while((s32[]{:T(128)}, f32[1536,128]{1,0:T(8,128)S(1)}, ...), condition=%wide.region_10.10_spmd, body=%wide.region_7.9_spmd.sunk | while | flops 274334208 | bytes 7905540 | solution.py:46
  124.4 7.1 %while.35 = (s32[]{:T(128)}, f32[1536,128]{1,0:T(8,128)S(1)}, s32[2]{0:T(128)S(1)}, s32[1536]{0:T(1024)S(1)}, s32[1024]{0:T(1024)S(1)}, /*index=5*/bf16[1024,128...) while((s32[]{:T(128)}, f32[1536,128]{1,0:T(8,128)S(1)}, ...), condition=%wide.region_10.10_spmd, body=%wide.region_7.9_spmd.sunk | while | flops 274334208 | bytes 7905540 | solution.py:46
  134.5 7.1 %while.35 = (s32[]{:T(128)}, f32[1536,128]{1,0:T(8,128)S(1)}, s32[2]{0:T(128)S(1)}, s32[1536]{0:T(1024)S(1)}, s32[1024]{0:T(1024)S(1)}, /*index=5*/bf16[1024,128...) while((s32[]{:T(128)}, f32[1536,128]{1,0:T(8,128)S(1)}, ...), condition=%wide.region_10.10_spmd, body=%wide.region_7.9_spmd.sunk | while | flops 274334208 | bytes 7905540 | solution.py:46
  142.3 3.0 %copy.208 = bf16[4,1024,128]{2,0,1:T(4,128)(2,1)} copy(bf16[4,1024,128]{2,1,0:T(8,128)(2,1)} %get-tuple-element.196) | data formatting | bytes 2097152 | tf_op jit(solution)/shard_map/while | solution.py:167
  145.3 4.2 %all-to-all-start.3 = ((bf16[1024,1,4,128]{3,2,1,0:T(4,128)(2,1)}), bf16[1024,1,4,128]{3,2,1,0:T(4,128)(2,1)S(1)}, u32[]{:S(2)}, u32[]{:S(2)}) async-start(bf16[1024,1,4,128]{3,2,1,0:T(4,128)(2,1)} %bitcast.126), calls=%async_computation.3 | async-start | bytes 2097152 | tf_op jit(solution)/shard_map/all_to_all | solution.py:169
  153.3 11.6 %all-to-all-done.3 = bf16[1024,1,4,128]{3,2,1,0:T(4,128)(2,1)S(1)} async-done(((bf16[1024,1,4,128]{3,2,1,0:T(4,128)(2,1)}), bf16[1024,1,4,128]{3,2,1,0:T(4,128)(2,1)S(1)}, u32[]{:S(2)}, u32[]{:S(2)}) %all-to-all-start.3) | async-done | bytes 1048608 | tf_op jit(solution)/shard_map/all_to_all | solution.py:169
  164.9 3.4 %all-to-all-start.5 = ((bf16[8,8,1024]{2,1,0:T(8,128)(2,1)}), bf16[8,8,1024]{2,1,0:T(8,128)(2,1)S(1)}, u32[]{:S(2)}, u32[]{:S(2)}) async-start(bf16[8,8,1024]{2,1,0:T(8,128)(2,1)} %copy.128), calls=%async_computation.5 | async-start | bytes 262144 | tf_op jit(solution)/shard_map/all_to_all | solution.py:149
  169.9 17.3 %reduce-scatter.2.cloned.1.call-done = f32[128,64]{0,1:T(8,128)} async-done(((f32[1024,64]{0,1:T(8,128)}), f32[128,64]{0,1:T(8,128)}) %reduce-scatter.2.cloned.1.call-update) | async-done | bytes 32784 | tf_op jit(solution)/shard_map/reduce_scatter | solution.py:138
  189.1 3.4 %all-to-all-start.9 = ((f32[1,64,1024]{2,0,1:T(1,128)}), f32[1,64,1024]{2,0,1:T(1,128)S(1)}, u32[]{:S(2)}, u32[]{:S(2)}) async-start(f32[1,64,1024]{2,0,1:T(1,128)} %copy.143), calls=%async_computation.10 | async-start | bytes 524288 | tf_op jit(solution)/shard_map/all_to_all | solution.py:192
  192.7 10.0 %all_gather.3 = bf16[1024,64]{0,1:T(8,128)(2,1)S(1)} all-gather(bf16[128,64]{0,1:T(8,128)(2,1)S(1)} %fusion.12), channel_id=1, replica_groups=mesh['seq'=8,'grp'=4] {'seq'}, dimensions={0}, use_global_device_ids=true | all-gather | bytes 147456 | tf_op jit(solution)/shard_map/all_gather | solution.py:183
  204.0 4.6 %all-to-all-start.10 = ((f32[4,2,8,1024]{3,1,2,0:T(2,128)}), f32[4,2,8,1024]{3,1,2,0:T(2,128)S(1)}, u32[]{:S(2)}, u32[]{:S(2)}) async-start(f32[4,2,8,1024]{3,1,2,0:T(2,128)} %fusion.22), calls=%async_computation.11 | async-start | bytes 524288 | tf_op jit(solution)/shard_map/all_to_all | solution.py:204
  212.1 5.9 %all-to-all-done.10 = f32[4,2,8,1024]{3,1,2,0:T(2,128)S(1)} async-done(((f32[4,2,8,1024]{3,1,2,0:T(2,128)}), f32[4,2,8,1024]{3,1,2,0:T(2,128)S(1)}, u32[]{:S(2)}, u32[]{:S(2)}) %all-to-all-start.10) | async-done | bytes 262176 | tf_op jit(solution)/shard_map/all_to_all | solution.py:204
  218.0 3.5 %all-to-all-start.7 = ((f32[4,2,64,512]{3,1,2,0:T(2,128)}), f32[4,2,64,512]{3,1,2,0:T(2,128)S(1)}, u32[]{:S(2)}, u32[]{:S(2)}) async-start(f32[4,2,64,512]{3,1,2,0:T(2,128)} %copy.134), calls=%async_computation.7 | async-start | bytes 2097152 | tf_op jit(solution)/shard_map/all_to_all | solution.py:197
  223.3 22.4 %all-to-all-done.7 = f32[4,2,64,512]{3,1,2,0:T(2,128)S(1)} async-done(((f32[4,2,64,512]{3,1,2,0:T(2,128)}), f32[4,2,64,512]{3,1,2,0:T(2,128)S(1)}, u32[]{:S(2)}, u32[]{:S(2)}) %all-to-all-start.7) | async-done | bytes 1048608 | tf_op jit(solution)/shard_map/all_to_all | solution.py:197
  245.7 2.6 %convolution_bitcast_fusion = f32[16,64,512]{2,0,1:T(8,128)S(1)} fusion(f32[4,2,64,512]{3,1,2,0:T(2,128)S(1)} %all-to-all-done.7, f32[4,2,16]{2,1,0:T(2,128)S(1)} %convert_reduce_fusion), kind=kOutput, calls=%fused_computation.21 | convolution fusion | flops 50331648 | bytes 3146240 | tf_op jit(solution)/shard_map/nca,ncrd->ard/dot_general | solution.py:212
  248.3 2.5 copy.148
  (152 shorter events, 64.6 us)
Async XLA Ops:
  7.2 38.4 %copy-start = (bf16[128,1024]{1,0:T(8,128)(2,1)S(1)}, bf16[128,1024]{1,0:T(8,128)(2,1)}, u32[]{:S(2)}) copy-start(bf16[128,1024]{1,0:T(8,128)(2,1)} %param.15) | copy-start | bytes 786436
  10.5 12.4 %all-to-all-start.4 = ((bf16[4,2,8,1024]{3,2,1,0:T(8,128)(2,1)}), bf16[4,2,8,1024]{3,2,1,0:T(8,128)(2,1)S(1)}, u32[]{:S(2)}, u32[]{:S(2)}) async-start(bf16[4,2,8,1024]{3,2,1,0:T(8,128)(2,1)} %copy.126), calls=%async_computation.4 | async-start | bytes 262144 | tf_op jit(solution)/shard_map/all_to_all | solution.py:107
  18.4 8.2 %copy-start.1 = (bf16[128,4096]{1,0:T(8,128)(2,1)S(1)}, bf16[128,4096]{1,0:T(8,128)(2,1)}, u32[]{:S(2)}) copy-start(bf16[128,4096]{1,0:T(8,128)(2,1)} %param.16) | copy-start | bytes 3145732
  22.9 19.1 %all-to-all-start = ((bf16[128,8,4,128]{3,0,2,1:T(8,128)(2,1)}), bf16[128,8,4,128]{3,0,2,1:T(8,128)(2,1)S(1)}, u32[]{:S(2)}, u32[]{:S(2)}) async-start(bf16[128,8,4,128]{3,0,2,1:T(8,128)(2,1)} %copy.115), calls=%async_computation | async-start | bytes 2097152 | tf_op jit(solution)/shard_map/all_to_all | solution.py:155
  42.0 18.9 %all-to-all-start.1 = ((bf16[128,8,4,128]{3,0,2,1:T(8,128)(2,1)}), bf16[128,8,4,128]{3,0,2,1:T(8,128)(2,1)S(1)}, u32[]{:S(2)}, u32[]{:S(2)}) async-start(bf16[128,8,4,128]{3,0,2,1:T(8,128)(2,1)} %copy.118), calls=%async_computation.1 | async-start | bytes 2097152 | tf_op jit(solution)/shard_map/all_to_all | solution.py:157
  62.2 18.9 %all-to-all-start.2 = ((bf16[128,8,4,128]{3,0,2,1:T(8,128)(2,1)}), bf16[128,8,4,128]{3,0,2,1:T(8,128)(2,1)S(1)}, u32[]{:S(2)}, u32[]{:S(2)}) async-start(bf16[128,8,4,128]{3,0,2,1:T(8,128)(2,1)} %broadcast_in_dim.80), calls=%async_computation.2 | async-start | bytes 2097152 | tf_op jit(solution)/shard_map/all_to_all | solution.py:156
  81.1 16.1 %all-to-all-start.8 = ((bf16[4,2,64,512]{3,2,1,0:T(8,128)(2,1)}), bf16[4,2,64,512]{3,2,1,0:T(8,128)(2,1)}, u32[]{:S(2)}, u32[]{:S(2)}) async-start(bf16[4,2,64,512]{3,2,1,0:T(8,128)(2,1)} %copy.139), calls=%async_computation.8 | async-start | bytes 1048576 | tf_op jit(solution)/shard_map/all_to_all | solution.py:106
  97.2 48.2 %all-to-all-start.6 = ((bf16[128,8,512]{2,0,1:T(8,128)(2,1)}), bf16[128,8,512]{2,0,1:T(8,128)(2,1)S(1)}, u32[]{:S(2)}, u32[]{:S(2)}) async-start(bf16[128,8,512]{2,0,1:T(8,128)(2,1)} %copy.130), calls=%async_computation.6 | async-start | bytes 2097152 | tf_op jit(solution)/shard_map/all_to_all | solution.py:134
  145.3 19.6 %all-to-all-start.3 = ((bf16[1024,1,4,128]{3,2,1,0:T(4,128)(2,1)}), bf16[1024,1,4,128]{3,2,1,0:T(4,128)(2,1)S(1)}, u32[]{:S(2)}, u32[]{:S(2)}) async-start(bf16[1024,1,4,128]{3,2,1,0:T(4,128)(2,1)} %bitcast.126), calls=%async_computation.3 | async-start | bytes 2097152 | tf_op jit(solution)/shard_map/all_to_all | solution.py:169
  149.5 37.6 %reduce-scatter.2.cloned.1.call-start = ((), (), s32[]{:S(2)}) async-start(), calls=%async_computation.12 | async-start | bytes 294912 | tf_op jit(solution)/shard_map/reduce_scatter | solution.py:138
  164.9 24.2 %all-to-all-start.5 = ((bf16[8,8,1024]{2,1,0:T(8,128)(2,1)}), bf16[8,8,1024]{2,1,0:T(8,128)(2,1)S(1)}, u32[]{:S(2)}, u32[]{:S(2)}) async-start(bf16[8,8,1024]{2,1,0:T(8,128)(2,1)} %copy.128), calls=%async_computation.5 | async-start | bytes 262144 | tf_op jit(solution)/shard_map/all_to_all | solution.py:149
  189.1 13.6 %all-to-all-start.9 = ((f32[1,64,1024]{2,0,1:T(1,128)}), f32[1,64,1024]{2,0,1:T(1,128)S(1)}, u32[]{:S(2)}, u32[]{:S(2)}) async-start(f32[1,64,1024]{2,0,1:T(1,128)} %copy.143), calls=%async_computation.10 | async-start | bytes 524288 | tf_op jit(solution)/shard_map/all_to_all | solution.py:192
  204.0 14.0 %all-to-all-start.10 = ((f32[4,2,8,1024]{3,1,2,0:T(2,128)}), f32[4,2,8,1024]{3,1,2,0:T(2,128)S(1)}, u32[]{:S(2)}, u32[]{:S(2)}) async-start(f32[4,2,8,1024]{3,1,2,0:T(2,128)} %fusion.22), calls=%async_computation.11 | async-start | bytes 524288 | tf_op jit(solution)/shard_map/all_to_all | solution.py:204
  218.0 27.7 %all-to-all-start.7 = ((f32[4,2,64,512]{3,1,2,0:T(2,128)}), f32[4,2,64,512]{3,1,2,0:T(2,128)S(1)}, u32[]{:S(2)}, u32[]{:S(2)}) async-start(f32[4,2,64,512]{3,1,2,0:T(2,128)} %copy.134), calls=%async_computation.7 | async-start | bytes 2097152 | tf_op jit(solution)/shard_map/all_to_all | solution.py:197
Sparse Core Ops, SparseCore 0:
  154.0 33.1 reduce-scatter.1
where the time goes:
time: 259 us; the launch traced here: 258 us
  waiting for transfers between devices  103 us (40%)
  local copies, waits for them, and re-layouts  45.5 us (18%)
  starting transfers between devices  45.3 us (17%)
  matrix products  25.1 us (10%)
  between operations  14.3 us (6%)
  blocking collectives  10 us (4%)
  other arithmetic  8.57 us (3%)
  loops' own time  5.43 us (2%)
    all_to_all x1, waiting for transfers between devices, local(): lax.all_to_all(slot_down.reshape(group_count, capacity, rank_overall, por...  22.4 us
    reduce_scatter x1, waiting for transfers between devices, local(): lax.psum_scatter(jnp.einsum('jyw,jaw->jya', token_rows, block_down_weight...  17.3 us
    all_to_all x1, waiting for transfers between devices, local(): lax.all_to_all(grad_grid, 'seq', split_axis=1, concat_axis=0, tiled=True)  15.3 us
    all_to_all x1, waiting for transfers between devices, local(): lax.all_to_all(query_grid, 'seq', split_axis=1, concat_axis=0, tiled=True)  13.4 us
    all_to_all x1, waiting for transfers between devices, local(): lax.all_to_all(key_grid, 'seq', split_axis=1, concat_axis=0, tiled=True)  12.5 us
    all_to_all x1, waiting for transfers between devices, local(): lax.all_to_all(head_grads, 'seq', split_axis=0, concat_axis=1, tiled=True)  11.6 us
    all_gather x1, blocking collectives, local(): lax.all_gather(backward_rank_part.reshape(tokens_here, rank_overall), 'se...  10 us
    unnamed x10, local copies, waits for them, and re-layouts  8.23 us
  transfers between devices with their start and end apart: 12, of which 9 were waited for; matrix products, arithmetic and copies ran while one was open for 26% of the time, Pallas kernels for 0%

commit v1 on v0

v1 whole, which is shorter than its diff:
```python
import functools
import math

import jax
import jax.numpy as jnp
from jax import lax
from jax.experimental import pallas as pl
from jax.experimental.pallas import tpu as pltpu
from jax.sharding import PartitionSpec as P

HEAD_DIM = 128
BLOCK = 128
SCALE = 2.0
MESH = pl.DeviceIdType.MESH
F32 = jnp.float32
BF16 = jnp.bfloat16


def segment_places(sai, row, seq, segs, resident, cap):
    owners, places, locals_ = [], [], []
    ranks = []
    for j in range(segs):
        slot = row[sai[seq, j]]
        owner = slot // resident
        rank = jnp.int32(0)
        for i in range(j):
            rank = rank + jnp.where(owners[i] == owner, 1, 0)
        owners.append(owner)
        ranks.append(rank)
        places.append(owner * cap + rank)
        locals_.append(slot - owner * resident)
    return owners, ranks, places, locals_


def chosen_rows(sai, row, group, sel, groups, segs, resident, cap, empty):
    def one(seq, carry):
        owners, ranks, _, held = segment_places(sai, row, seq, segs, resident, cap)
        for c in range(cap):
            value = jnp.int32(empty)
            for j in range(segs):
                value = jnp.where((owners[j] == group) & (ranks[j] == c), held[j], value)
            sel[seq * cap + c] = value
        return carry

    lax.fori_loop(0, groups, one, 0)


def exchange_kernel(
    cfg, sai, cnt, row, x, q, k, o, ad, au, down_out, up_out,
    seg_s, place_s, sel_s,
    qb, ob, kb, xb, adv, auv, asend, usend, acand, ucand, u2send, u2, uf,
    lowsend, lowr, vgsend, vgr, blr, utsend, utr, dsend, tf, tsend, acc,
    seq_send, seq_recv, grp_send, grp_recv, near,
):
    n, groups, cap, segs, resident, rank, rp, fw, hh, gs, reach, pad = cfg
    s = lax.axis_index("seq")
    g = lax.axis_index("grp")
    hw = hh * HEAD_DIM
    blk = BLOCK

    def lanes(index, width):
        return pl.ds(pl.multiple_of(index * width, 128), width)

    def seq_copy(kind, src, dst, peer, origin):
        return pltpu.make_async_remote_copy(
            src_ref=src, dst_ref=dst, send_sem=seq_send.at[kind, peer],
            recv_sem=seq_recv.at[kind, origin], device_id={"seq": peer}, device_id_type=MESH)

    def grp_copy(kind, src, dst, peer, origin):
        return pltpu.make_async_remote_copy(
            src_ref=src, dst_ref=dst, send_sem=grp_send.at[kind, peer],
            recv_sem=grp_recv.at[kind, origin], device_id={"grp": peer}, device_id_type=MESH)

    def key_src(p):
        return k.at[:, lanes((p * hh) // gs, HEAD_DIM)]

    seq_kinds = {
        "k": (0, key_src, lambda i: kb.at[pad + i]),
        "q": (1, lambda p: q.at[:, lanes(p, hw)], lambda i: qb.at[i]),
        "o": (2, lambda p: o.at[:, lanes(p, hw)], lambda i: ob.at[i]),
        "x": (3, lambda p: x.at[:, lanes(p, fw)], lambda i: xb.at[i]),
        "u": (4, lambda p: u2send.at[p], lambda i: u2.at[i]),
        "low": (5, lambda p: lowsend.at[p], lambda i: lowr.at[i]),
        "vg": (6, lambda p: vgsend.at[p], lambda i: vgr.at[i]),
        "bl": (7, lambda p: blr.at[s], lambda i: blr.at[i]),
        "ut": (8, lambda p: utsend.at[p], lambda i: utr.at[i]),
    }
    grp_kinds = {
        "a": (0, lambda p: asend.at[pl.ds(p * cap, cap)], lambda i: acand.at[pl.ds(i * cap, cap)]),
        "b": (1, lambda p: usend.at[pl.ds(p * cap, cap)], lambda i: ucand.at[pl.ds(i * cap, cap)]),
        "d": (2, lambda p: dsend.at[p], lambda i: down_out.at[i]),
        "t": (3, lambda p: tsend.at[p], lambda i: up_out.at[i]),
    }

    def send_one(name, peer):
        kind, src, dst = seq_kinds[name]
        seq_copy(kind, src(peer), dst(s), peer, s).start()

    def wait_one(name, origin):
        kind, src, dst = seq_kinds[name]
        seq_copy(kind, src(origin), dst(origin), origin, origin).wait_recv()

    def each_peer(fn, me, count):
        def body(step, carry):
            fn(lax.rem(me + step, count))
            return carry
        lax.fori_loop(1, count, body, 0)

    def send_seq(name):
        each_peer(lambda p: send_one(name, p), s, n)

    def wait_seq(name):
        each_peer(lambda p: wait_one(name, p), s, n)

    def sent_seq(name):
        kind, src, dst = seq_kinds[name]
        each_peer(lambda p: seq_copy(kind, src(p), dst(s), p, s).wait_send(), s, n)

    def send_grp_one(name, peer):
        kind, src, dst = grp_kinds[name]
        grp_copy(kind, src(peer), dst(g), peer, g).start()

    def wait_grp(name):
        kind, src, dst = grp_kinds[name]
        each_peer(lambda p: grp_copy(kind, src(p), dst(p), p, p).wait_recv(), g, groups)

    def sent_grp(name):
        kind, src, dst = grp_kinds[name]
        each_peer(lambda p: grp_copy(kind, src(p), dst(g), p, g).wait_send(), g, groups)

    barrier = pltpu.get_barrier_semaphore()

    def greet_seq(p):
        pl.semaphore_signal(barrier, inc=1, device_id={"seq": p}, device_id_type=MESH)

    def greet_grp(p):
        pl.semaphore_signal(barrier, inc=1, device_id={"grp": p}, device_id_type=MESH)

    each_peer(greet_seq, s, n)
    each_peer(greet_grp, g, groups)

    own = {}
    for number, name in enumerate(("k", "q", "o", "x")):
        _, src, dst = seq_kinds[name]
        own[name] = pltpu.make_async_copy(src(s), dst(s), near.at[number])
    own["a"] = pltpu.make_async_copy(ad, adv, near.at[4])
    own["b"] = pltpu.make_async_copy(au, auv, near.at[5])
    for name in ("a", "b", "k", "q", "o", "x"):
        own[name].start()

    chosen_rows(sai, row, g, sel_s, groups, segs, resident, cap, 0)
    owners, ranks, places, _ = segment_places(sai, row, g, segs, resident, cap)
    ends = []
    total = jnp.int32(0)
    for j in range(segs):
        total = total + cnt[g, j]
        ends.append(total)
    for b in range(pad):
        seg_s[b] = jnp.int32(-1)

    def one_block(b, carry):
        seg = jnp.int32(0)
        for j in range(segs):
            seg = seg + jnp.where(b >= ends[j], 1, 0)
        place = jnp.int32(0)
        for j in range(segs):
            place = jnp.where(seg == j, places[j], place)
        seg_s[pad + b] = seg
        place_s[b] = place
        return carry

    lax.fori_loop(0, n, one_block, 0)

    pl.semaphore_wait(barrier, n - 1 + groups - 1)
    send_seq("k")
    for_heads = ("q", "o")

    def send_heads(p):
        for name in for_heads:
            send_one(name, p)

    each_peer(send_heads, s, n)

    own["a"].wait()
    own["b"].wait()

    def pick(slot, carry):
        index = sel_s[slot]
        asend[slot] = adv[index]
        usend[slot] = auv[index]
        return carry

    lax.fori_loop(0, groups * cap, pick, 0)
    each_peer(lambda p: send_grp_one("b", p), g, groups)
    each_peer(lambda p: send_grp_one("a", p), g, groups)
    send_seq("x")
    for c in range(cap):
        acand[g * cap + c] = asend[g * cap + c]
        ucand[g * cap + c] = usend[g * cap + c]
    for b in range(pad):
        kb[b] = jnp.zeros_like(kb[b])
    acc[...] = jnp.zeros_like(acc)

    wait_grp("b")

    def route(b, carry):
        u2send[b] = ucand[place_s[b]]
        return carry

    lax.fori_loop(0, n, route, 0)
    send_seq("u")
    u2[s] = u2send[s]

    factor = math.log2(math.e) / math.sqrt(HEAD_DIM)

    def attend(b, first, count):
        width = count * blk
        queries = jnp.concatenate(
            [qb[b, :, h * HEAD_DIM:(h + 1) * HEAD_DIM] for h in range(hh)], 0)
        grads = jnp.concatenate(
            [ob[b, :, h * HEAD_DIM:(h + 1) * HEAD_DIM] for h in range(hh)], 0)
        keys = kb[pl.ds(first, count)].reshape(width, HEAD_DIM)
        scores = lax.dot_general(queries, keys, (((1,), (1,)), ((), ())),
                                 preferred_element_type=F32)
        column = lax.broadcasted_iota(jnp.int32, (1, width), 1)
        ids = jnp.full((1, width), seg_s[first], jnp.int32)
        for j in range(1, count):
            ids = jnp.where(column >= j * blk, seg_s[first + j], ids)
        rows = lax.broadcasted_iota(jnp.int32, (blk, width), 0)
        columns = lax.broadcasted_iota(jnp.int32, (blk, width), 1)
        seen = (ids == seg_s[pad + b]) & (columns - (count - 1) * blk <= rows)
        bias = jnp.where(seen, F32(0), F32(-1e30))
        scores = (scores.reshape(hh, blk, width) + bias[None]).reshape(hh * blk, width)
        highest = jnp.max(scores, axis=1, keepdims=True)
        expo = jnp.exp2((scores - highest) * factor)
        probs = (expo * (1.0 / jnp.sum(expo, axis=1, keepdims=True))).astype(BF16)
        part = lax.dot_general(probs, grads, (((0,), (0,)), ((), ())),
                               preferred_element_type=F32)
        acc[pl.ds(first, count)] += part.reshape(count, blk, HEAD_DIM)

    def arrived(b):
        @pl.when(b != s)
        def _():
            for name in ("k", "q", "o"):
                wait_one(name, b)

        @pl.when(b == s)
        def _():
            for name in ("k", "q", "o"):
                own[name].wait()

    def finish(b):
        vgsend[b] = acc[pad + b].astype(BF16)

        @pl.when(b != s)
        def _():
            send_one("vg", b)

        @pl.when(b == s)
        def _():
            vgr[s] = vgsend[b]

    if pad == 0:
        for b in range(n):
            arrived(b)
            attend(b, max(b - reach + 1, 0), min(b + 1, reach))
            if b >= reach - 1:
                finish(b - reach + 1)
        for b in range(n - reach + 1, n):
            finish(b)
    else:
        def step(b, carry):
            arrived(b)
            attend(b, b, reach)
            return carry

        lax.fori_loop(0, n, step, 0)

        def last(b, carry):
            finish(b)
            return carry

        lax.fori_loop(0, n, last, 0)

    wait_seq("u")
    for i in range(n):
        uf[i * rp:(i + 1) * rp, :] = u2[i].astype(F32)
    up_rows = uf[...].astype(BF16)
    wait_seq("vg")
    share = gs // hh
    heads = []
    for kv in range(n // share):
        if share == 1:
            heads.append(vgr[kv])
        else:
            whole = vgr[kv * share].astype(F32)
            for i in range(1, share):
                whole = whole + vgr[kv * share + i].astype(F32)
            heads.append(whole.astype(BF16))
    value_grad = jnp.concatenate(heads, 1)
    back = SCALE * lax.dot_general(up_rows, value_grad, (((1,), (1,)), ((), ())),
                                   preferred_element_type=F32)
    blr[s] = back.astype(BF16)
    send_seq("bl")

    wait_grp("a")
    own["x"].wait()
    wait_seq("x")

    def lowered(b, carry):
        lowsend[b] = lax.dot_general(acand[place_s[b]], xb[b], (((1,), (1,)), ((), ())),
                                     preferred_element_type=F32)
        return carry

    lax.fori_loop(0, n, lowered, 0)
    send_seq("low")
    lowr[s] = lowsend[s]

    wait_seq("bl")
    features = xb[...].reshape(n * blk, fw)

    def down_terms(peer):
        rows = []
        for c in range(cap):
            rows.append(jnp.concatenate(
                [jnp.where(place_s[b] == peer * cap + c, blr[b].astype(F32), F32(0)).astype(BF16)
                 for b in range(n)], 1))
        dsend[peer] = lax.dot_general(jnp.concatenate(rows, 0), features,
                                      (((1,), (0,)), ((), ())),
                                      preferred_element_type=F32).astype(BF16)

    def down_send(peer):
        down_terms(peer)
        send_grp_one("d", peer)

    each_peer(down_send, g, groups)
    down_terms(g)
    mine_down = pltpu.make_async_copy(dsend.at[g], down_out.at[g], near.at[6])
    mine_down.start()

    wait_seq("low")
    low = lowr[0]
    for i in range(1, n):
        low = low + lowr[i]
    terms = SCALE * lax.dot_general(low.astype(BF16), value_grad, (((1,), (0,)), ((), ())),
                                    preferred_element_type=F32)
    for i in range(n):
        utsend[i] = terms[i * rp:(i + 1) * rp, :]
    send_seq("ut")
    utr[s] = utsend[s]
    wait_seq("ut")

    def up_terms(peer):
        for c in range(cap):
            def add(b, total):
                return total + jnp.where(place_s[b] == peer * cap + c, utr[b], F32(0))
            tf[c * rp:(c + 1) * rp, :] = lax.fori_loop(
                0, n, add, jnp.zeros(utr.shape[1:], F32))
        tsend[peer] = tf[...].astype(BF16)

    def up_send(peer):
        up_terms(peer)
        send_grp_one("t", peer)

    each_peer(up_send, g, groups)
    up_terms(g)
    mine_up = pltpu.make_async_copy(tsend.at[g], up_out.at[g], near.at[7])
    mine_up.start()

    for name in seq_kinds:
        sent_seq(name)
    for name in grp_kinds:
        sent_grp(name)
    mine_down.wait()
    mine_up.wait()
    wait_grp("d")
    wait_grp("t")


def spread_kernel(cfg, sai, row, down, up, down_grad, up_grad, sel_s):
    groups, cap, segs, resident, rank, rp = cfg
    step = pl.program_id(0)
    here = down_grad.shape[0]
    g = lax.axis_index("grp")

    @pl.when(step == 0)
    def _():
        chosen_rows(sai, row, g, sel_s, groups, segs, resident, cap, -1)

    def rows_of(terms, ranks):
        count = groups * cap
        slots = lax.broadcasted_iota(jnp.int32, (1, count * ranks), 1)
        target = jnp.full((1, count * ranks), -1, jnp.int32)
        for i in range(count):
            inside = (slots >= i * ranks) & (slots < (i + 1) * ranks)
            first = jnp.where(sel_s[i] < 0, -(1 << 20), (sel_s[i] - step * here) * ranks)
            target = jnp.where(inside, first + slots - i * ranks, target)
        rows = lax.broadcasted_iota(jnp.int32, (here * ranks, count * ranks), 0)
        onehot = jnp.where(rows == target, F32(1), F32(0)).astype(BF16)
        return lax.dot_general(onehot, terms, (((1,), (0,)), ((), ())), preferred_element_type=F32)

    down_grad[...] = rows_of(down[...], rank).reshape(down_grad.shape)
    up_grad[...] = rows_of(up[...], rp).reshape(up_grad.shape)


def local(x, q, k, o, ad, au, sai, cnt, row):
    groups = lax.axis_size("grp")
    n = lax.axis_size("seq")
    tokens = x.shape[0]
    fw = ad.shape[2]
    resident, rank = ad.shape[0], ad.shape[1]
    rp, vw = au.shape[1], au.shape[2]
    segs = sai.shape[1]
    cap = max(2, (segs + groups - 1) // groups)
    reach = min(16, n * tokens // (2 * BLOCK))
    heads = q.shape[1] // HEAD_DIM
    hh = heads // n
    gs = heads // (vw // HEAD_DIM)
    assert tokens == BLOCK and gs % hh == 0
    pad = 0 if n <= 8 else reach - 1
    cfg = (n, groups, cap, segs, resident, rank, rp, fw, hh, gs, reach, pad)
    slots = groups * cap
    smem = pl.BlockSpec(memory_space=pltpu.SMEM)
    hbm = pl.BlockSpec(memory_space=pl.ANY)
    down, up = pl.pallas_call(
        functools.partial(exchange_kernel, cfg),
        out_shape=(
            jax.ShapeDtypeStruct((groups, cap * rank, fw), BF16),
            jax.ShapeDtypeStruct((groups, cap * rp, vw), BF16),
        ),
        in_specs=[smem] * 3 + [hbm] * 6,
        out_specs=(hbm, hbm),
        scratch_shapes=[
            pltpu.SMEM((n + pad,), jnp.int32),
            pltpu.SMEM((n,), jnp.int32),
            pltpu.SMEM((slots,), jnp.int32),
            pltpu.VMEM((n, BLOCK, hh * HEAD_DIM), BF16),
            pltpu.VMEM((n, BLOCK, hh * HEAD_DIM), BF16),
            pltpu.VMEM((n + pad, BLOCK, HEAD_DIM), BF16),
            pltpu.VMEM((n, BLOCK, fw), BF16),
            pltpu.VMEM(ad.shape, BF16),
            pltpu.VMEM(au.shape, BF16),
            pltpu.VMEM((slots, rank, fw), BF16),
            pltpu.VMEM((slots, rp, vw), BF16),
            pltpu.VMEM((slots, rank, fw), BF16),
            pltpu.VMEM((slots, rp, vw), BF16),
            pltpu.VMEM((n, rp, vw), BF16),
            pltpu.VMEM((n, rp, vw), BF16),
            pltpu.VMEM((rank, vw), F32),
            pltpu.VMEM((n, rank, BLOCK), F32),
            pltpu.VMEM((n, rank, BLOCK), F32),
            pltpu.VMEM((n, BLOCK, HEAD_DIM), BF16),
            pltpu.VMEM((n, BLOCK, HEAD_DIM), BF16),
            pltpu.VMEM((n, rank, BLOCK), BF16),
            pltpu.VMEM((n, rp, vw), F32),
            pltpu.VMEM((n, rp, vw), F32),
            pltpu.VMEM((groups, cap * rank, fw), BF16),
            pltpu.VMEM((cap * rp, vw), F32),
            pltpu.VMEM((groups, cap * rp, vw), BF16),
            pltpu.VMEM((n + pad, BLOCK, HEAD_DIM), F32),
            pltpu.SemaphoreType.DMA((9, n)),
            pltpu.SemaphoreType.DMA((9, n)),
            pltpu.SemaphoreType.DMA((4, groups)),
            pltpu.SemaphoreType.DMA((4, groups)),
            pltpu.SemaphoreType.DMA((8,)),
        ],
        compiler_params=pltpu.CompilerParams(
            collective_id=0, has_side_effects=True, vmem_limit_bytes=40 * 1024 * 1024),
        name="exchange",
    )(sai, cnt, row, x, q, k, o, ad, au)
    steps = 4
    here = resident // steps
    return pl.pallas_call(
        functools.partial(spread_kernel, (groups, cap, segs, resident, rank, rp)),
        grid=(steps,),
        out_shape=(
            jax.ShapeDtypeStruct((resident, rank, fw), F32),
            jax.ShapeDtypeStruct((resident, rp, vw), F32),
        ),
        in_specs=[
            smem, smem,
            pl.BlockSpec((slots * rank, fw), lambda i: (0, 0)),
            pl.BlockSpec((slots * rp, vw), lambda i: (0, 0)),
        ],
        out_specs=(
            pl.BlockSpec((here, rank, fw), lambda i: (i, 0, 0)),
            pl.BlockSpec((here, rp, vw), lambda i: (i, 0, 0)),
        ),
        scratch_shapes=[pltpu.SMEM((slots,), jnp.int32)],
        compiler_params=pltpu.CompilerParams(vmem_limit_bytes=40 * 1024 * 1024),
        name="spread",
    )(sai, row, down.reshape(slots * rank, fw), up.reshape(slots * rp, vw))


def solution(mesh):
    return jax.shard_map(
        local,
        mesh=mesh,
        in_specs=(
            P(("grp", "seq"), None),
            P(("grp", "seq"), None),
            P(("grp", "seq"), None),
            P(("grp", "seq"), None),
            P("grp", None, "seq"),
            P("grp", "seq", None),
            P(),
            P(),
            P(),
        ),
        out_specs=(P("grp", None, "seq"), P("grp", "seq", None)),
        check_vma=False,
    )
```

time: 259 us -> 84 us (0.32)
  waiting for transfers between devices: 103 us -> 0 us
  Pallas kernels: 0 us -> 74.1 us
  starting transfers between devices: 45.3 us -> 0 us
  local copies, waits for them, and re-layouts: 45.5 us -> 8.81 us
  matrix products: 25.1 us -> 0 us
  between operations: 14.3 us -> 0.66 us
  blocking collectives: 10 us -> 0 us
  other arithmetic: 8.57 us -> 0 us
  loops' own time: 5.43 us -> 0 us
    all_to_all x11 -> x0, waiting for transfers between devices: 86.2 us -> none  [the longest x1 22.4 us: local(): lax.all_to_all(slot_down.reshape(group_count, capacity, rank_overall, por...]
    pallas_call x0 -> x2, Pallas kernels: none -> 74.1 us  [the longest x1 70.7 us: local(): pl.pallas_call(functools.partial(exchange_kernel, cfg), out_shape=(jax.Sh...]
    all_to_all x11 -> x0, starting transfers between devices: 45.3 us -> none  [the longest x1 6.32 us: local(): lax.all_to_all(send_up, 'grp', split_axis=0, concat_axis=0, tiled=True)]
    dot_general x28 -> x0, matrix products: 25.1 us -> none  [the longest x8 6.67 us: one_block(): jnp.dot(probabilities.T, grad_block, preferred_element_type=jnp.float32)]
    reduce_scatter x1 -> x0, waiting for transfers between devices: 17.3 us -> none  [local(): lax.psum_scatter(jnp.einsum('jyw,jaw->jya', token_rows, block_down_weight...]
    all_gather x1 -> x0, blocking collectives: 10 us -> none  [local(): lax.all_gather(backward_rank_part.reshape(tokens_here, rank_overall), 'se...]
    squeeze x8 -> x0, local copies, waits for them, and re-layouts: 8.15 us -> none  [local(): result = lax.map(per_head, stacked)]
    reduce_sum x14 -> x0, other arithmetic: 7.57 us -> none  [the longest x8 4.12 us: one_block(): jnp.sum(expo, axis=1, keepdims=True)]
  transfers between devices with their start and end apart: 12 -> 0, of which waited for: 9 -> 0; matrix products, arithmetic and copies ran while one was open for 26% -> 0% of each run, Pallas kernels for 0% -> 0%
where the time goes in v1:
time: 84 us; the launch traced here: 83.6 us
  Pallas kernels  74.1 us (88%)
  local copies, waits for them, and re-layouts  8.81 us (10%)
    pallas_call x1, Pallas kernels, local(): pl.pallas_call(functools.partial(exchange_kernel, cfg), out_shape=(jax.Sh...  70.7 us
    unnamed x18, local copies, waits for them, and re-layouts  8.81 us
    pallas_call x1, Pallas kernels, local(): pl.pallas_call(functools.partial(spread_kernel, (groups, cap, segs, resid...  3.42 us

profile of v1, /device:TPU:0, one launch (start us, length us, event | category | flops | bytes accessed | tf_op | source)
XLA Modules:
  0.0 83.6 jit_solution(15953173081259251638)
XLA Ops:
  0.6 0.0 copy-start
  0.6 1.2 %copy-done = bf16[128,4096]{1,0:T(8,128)(2,1)S(1)} copy-done((bf16[128,4096]{1,0:T(8,128)(2,1)S(1)}, bf16[128,4096]{1,0:T(8,128)(2,1)}, u32[]{:S(2)}) %copy-start) | copy-done | bytes 1048600
  1.9 0.0 copy-start.1
  1.9 1.2 %copy-done.1 = bf16[128,4096]{1,0:T(8,128)(2,1)S(1)} copy-done((bf16[128,4096]{1,0:T(8,128)(2,1)S(1)}, bf16[128,4096]{1,0:T(8,128)(2,1)}, u32[]{:S(2)}) %copy-start.1) | copy-done | bytes 1048600
  3.1 0.0 copy-start.2
  3.1 1.2 %copy-done.2 = bf16[128,4096]{1,0:T(8,128)(2,1)S(1)} copy-done((bf16[128,4096]{1,0:T(8,128)(2,1)S(1)}, bf16[128,4096]{1,0:T(8,128)(2,1)}, u32[]{:S(2)}) %copy-start.2) | copy-done | bytes 1048600
  4.3 0.0 copy-start.3
  4.3 1.2 %copy-done.3 = bf16[16,64,512]{2,1,0:T(8,128)(2,1)S(1)} copy-done((bf16[16,64,512]{2,1,0:T(8,128)(2,1)S(1)}, bf16[16,64,512]{2,1,0:T(8,128)(2,1)}, u32[]{:S(2)}) %copy-start.3) | copy-done | bytes 1048600
  5.5 0.0 copy-start.4
  5.5 0.9 %copy-done.4 = bf16[128,1024]{1,0:T(8,128)(2,1)S(1)} copy-done((bf16[128,1024]{1,0:T(8,128)(2,1)S(1)}, bf16[128,1024]{1,0:T(8,128)(2,1)}, u32[]{:S(2)}) %copy-start.4) | copy-done | bytes 262168
  6.5 0.0 copy-start.5
  6.5 0.9 %copy-done.5 = bf16[16,8,1024]{2,1,0:T(8,128)(2,1)S(1)} copy-done((bf16[16,8,1024]{2,1,0:T(8,128)(2,1)S(1)}, bf16[16,8,1024]{2,1,0:T(8,128)(2,1)}, u32[]{:S(2)}) %copy-start.5) | copy-done | bytes 262168
  7.4 0.0 copy-start.6
  7.4 0.7 copy-done.6
  8.1 0.0 copy-start.7
  8.1 0.7 copy-done.7
  8.8 0.0 copy-start.8
  8.8 0.7 copy-done.8
  9.5 70.7 %exchange.1 = (bf16[4,128,512]{2,1,0:T(8,128)(2,1)S(1)}, bf16[4,16,1024]{2,1,0:T(8,128)(2,1)S(1)}) custom-call(s32[4,4]{1,0:T(4,128)S(1)} %copy-done.6, s32[4,4]{1,0:T(4,128)S(1)} %copy-done.7, s32[64]{0:T(128)S(1)} %copy-done.8, bf16[128,4096]{1,0:T(8,128)(2,1)S(1)} %copy-done, bf16[128,4096]{1,0:T(8,128)(2,1)S(1)} %copy-done.1, ...), custom_call_target="tpu_custom_call" | custom-call | tf_op jit(solution)/shard_map/exchange/pallas_call | solution.py:425
  80.2 3.4 %spread.1 = (f32[16,64,512]{2,1,0:T(8,128)}, f32[16,8,1024]{2,1,0:T(8,128)}) custom-call(s32[4,4]{1,0:T(4,128)S(1)} %copy-done.6, s32[64]{0:T(128)S(1)} %copy-done.8, bf16[512,512]{1,0:T(8,128)(2,1)S(1)} %bitcast.2, bf16[64,1024]{1,0:T(8,128)(2,1)S(1)} %bitcast.3), custom_call_target="tpu_custom_call" | custom-call | tf_op jit(solution)/shard_map/spread/pallas_call | solution.py:473
Async XLA Ops:
  0.6 1.2 %copy-start = (bf16[128,4096]{1,0:T(8,128)(2,1)S(1)}, bf16[128,4096]{1,0:T(8,128)(2,1)}, u32[]{:S(2)}) copy-start(bf16[128,4096]{1,0:T(8,128)(2,1)} %x.1) | copy-start | bytes 3145732
  1.9 1.2 %copy-start.1 = (bf16[128,4096]{1,0:T(8,128)(2,1)S(1)}, bf16[128,4096]{1,0:T(8,128)(2,1)}, u32[]{:S(2)}) copy-start(bf16[128,4096]{1,0:T(8,128)(2,1)} %q.1) | copy-start | bytes 3145732
  3.1 1.2 %copy-start.2 = (bf16[128,4096]{1,0:T(8,128)(2,1)S(1)}, bf16[128,4096]{1,0:T(8,128)(2,1)}, u32[]{:S(2)}) copy-start(bf16[128,4096]{1,0:T(8,128)(2,1)} %o.1) | copy-start | bytes 3145732
  4.3 1.2 %copy-start.3 = (bf16[16,64,512]{2,1,0:T(8,128)(2,1)S(1)}, bf16[16,64,512]{2,1,0:T(8,128)(2,1)}, u32[]{:S(2)}) copy-start(bf16[16,64,512]{2,1,0:T(8,128)(2,1)} %ad.1) | copy-start | bytes 3145732
  5.5 0.9 %copy-start.4 = (bf16[128,1024]{1,0:T(8,128)(2,1)S(1)}, bf16[128,1024]{1,0:T(8,128)(2,1)}, u32[]{:S(2)}) copy-start(bf16[128,1024]{1,0:T(8,128)(2,1)} %k.1) | copy-start | bytes 786436
  6.5 0.9 %copy-start.5 = (bf16[16,8,1024]{2,1,0:T(8,128)(2,1)S(1)}, bf16[16,8,1024]{2,1,0:T(8,128)(2,1)}, u32[]{:S(2)}) copy-start(bf16[16,8,1024]{2,1,0:T(8,128)(2,1)} %au.1) | copy-start | bytes 786436
  7.4 0.7 copy-start.6
  8.1 0.7 copy-start.7
  8.8 0.7 copy-start.8

commit v2 on v1

--- a/solution.py
+++ b/solution.py
@@ -171,15 +171,24 @@
 
     lax.fori_loop(0, n, one_block, 0)
 
+    def partner(step):
+        index, bit = 0, 1
+        while bit < n:
+            ours, flip = (s // bit) % 2, (step // bit) % 2
+            index = index + (ours + flip - 2 * ours * flip) * bit
+            bit *= 2
+        return index
+
+    def send_heads(p):
+        for name in ("q", "o"):
+            send_one(name, p)
+
+    order = [1, 2, 4, 6, 3, 5, 7] if n == 8 else list(range(1, n))
+    ahead = min(4, n - 1)
     pl.semaphore_wait(barrier, n - 1 + groups - 1)
     send_seq("k")
-    for_heads = ("q", "o")
-
-    def send_heads(p):
-        for name in for_heads:
-            send_one(name, p)
-
-    each_peer(send_heads, s, n)
+    for step in order[:ahead]:
+        send_heads(partner(step))
 
     own["a"].wait()
     own["b"].wait()
@@ -193,7 +202,6 @@
     lax.fori_loop(0, groups * cap, pick, 0)
     each_peer(lambda p: send_grp_one("b", p), g, groups)
     each_peer(lambda p: send_grp_one("a", p), g, groups)
-    send_seq("x")
     for c in range(cap):
         acand[g * cap + c] = asend[g * cap + c]
         ucand[g * cap + c] = usend[g * cap + c]
@@ -201,15 +209,15 @@
         kb[b] = jnp.zeros_like(kb[b])
     acc[...] = jnp.zeros_like(acc)
 
-    wait_grp("b")
-
     def route(b, carry):
         u2send[b] = ucand[place_s[b]]
         return carry
 
-    lax.fori_loop(0, n, route, 0)
-    send_seq("u")
-    u2[s] = u2send[s]
+    def route_up():
+        wait_grp("b")
+        lax.fori_loop(0, n, route, 0)
+        send_seq("u")
+        u2[s] = u2send[s]
 
     factor = math.log2(math.e) / math.sqrt(HEAD_DIM)
 
@@ -238,49 +246,52 @@
                                preferred_element_type=F32)
         acc[pl.ds(first, count)] += part.reshape(count, blk, HEAD_DIM)
 
-    def arrived(b):
-        @pl.when(b != s)
-        def _():
-            for name in ("k", "q", "o"):
-                wait_one(name, b)
-
-        @pl.when(b == s)
-        def _():
-            for name in ("k", "q", "o"):
-                own[name].wait()
-
-    def finish(b):
+    own["k"].wait()
+    own["q"].wait()
+    own["o"].wait()
+    wait_seq("k")
+    attend(s, s, reach)
+
+    def visit(b):
+        wait_one("q", b)
+        wait_one("o", b)
+        attend(b, b, reach)
+
+    early = 0
+    if n == 8:
+        for number, step in enumerate(order):
+            if number >= 1 and number - 1 + ahead < n - 1:
+                send_heads(partner(order[number - 1 + ahead]))
+            if number == 2:
+                route_up()
+            if number == 4:
+                early = 4
+                for other in order[:early]:
+                    send_one("x", partner(other))
+            visit(partner(step))
+    else:
+        route_up()
+
+        def one_step(step, carry):
+            @pl.when(step + ahead < n)
+            def _():
+                send_heads(partner(step + ahead))
+
+            visit(partner(step))
+            return carry
+
+        lax.fori_loop(1, n, one_step, 0)
+
+    def finish(step, carry):
+        b = partner(step)
         vgsend[b] = acc[pad + b].astype(BF16)
-
-        @pl.when(b != s)
-        def _():
-            send_one("vg", b)
-
-        @pl.when(b == s)
-        def _():
-            vgr[s] = vgsend[b]
-
-    if pad == 0:
-        for b in range(n):
-            arrived(b)
-            attend(b, max(b - reach + 1, 0), min(b + 1, reach))
-            if b >= reach - 1:
-                finish(b - reach + 1)
-        for b in range(n - reach + 1, n):
-            finish(b)
-    else:
-        def step(b, carry):
-            arrived(b)
-            attend(b, b, reach)
-            return carry
-
-        lax.fori_loop(0, n, step, 0)
-
-        def last(b, carry):
-            finish(b)
-            return carry
-
-        lax.fori_loop(0, n, last, 0)
+        send_one("vg", b)
+        return carry
+
+    lax.fori_loop(1, n, finish, 0)
+    vgr[s] = acc[pad + s].astype(BF16)
+    for step in order[early:]:
+        send_one("x", partner(step))
 
     wait_seq("u")
     for i in range(n):
@@ -416,8 +427,8 @@
     heads = q.shape[1] // HEAD_DIM
     hh = heads // n
     gs = heads // (vw // HEAD_DIM)
-    assert tokens == BLOCK and gs % hh == 0
-    pad = 0 if n <= 8 else reach - 1
+    assert tokens == BLOCK and gs % hh == 0 and n & (n - 1) == 0
+    pad = reach - 1
     cfg = (n, groups, cap, segs, resident, rank, rp, fw, hh, gs, reach, pad)
     slots = groups * cap
     smem = pl.BlockSpec(memory_space=pltpu.SMEM)
@@ -428,7 +439,7 @@
             jax.ShapeDtypeStruct((groups, cap * rank, fw), BF16),
             jax.ShapeDtypeStruct((groups, cap * rp, vw), BF16),
         ),
-        in_specs=[smem] * 3 + [hbm] * 6,
+        in_specs=[smem] * 3 + [pl.BlockSpec(memory_space=pltpu.HBM)] * 6,
         out_specs=(hbm, hbm),
         scratch_shapes=[
             pltpu.SMEM((n + pad,), jnp.int32),
@@ -465,7 +476,7 @@
             pltpu.SemaphoreType.DMA((8,)),
         ],
         compiler_params=pltpu.CompilerParams(
-            collective_id=0, has_side_effects=True, vmem_limit_bytes=40 * 1024 * 1024),
+            collective_id=0, has_side_effects=True, vmem_limit_bytes=60 * 1024 * 1024),
         name="exchange",
     )(sai, cnt, row, x, q, k, o, ad, au)
     steps = 4
@@ -487,7 +498,7 @@
             pl.BlockSpec((here, rp, vw), lambda i: (i, 0, 0)),
         ),
         scratch_shapes=[pltpu.SMEM((slots,), jnp.int32)],
-        compiler_params=pltpu.CompilerParams(vmem_limit_bytes=40 * 1024 * 1024),
+        compiler_params=pltpu.CompilerParams(vmem_limit_bytes=60 * 1024 * 1024),
         name="spread",
     )(sai, row, down.reshape(slots * rank, fw), up.reshape(slots * rp, vw))
 

time: 84 us -> 73.2 us (0.87)
  local copies, waits for them, and re-layouts: 8.81 us -> 0 us
  Pallas kernels: 74.1 us -> 72.3 us
    unnamed x18 -> x0, local copies, waits for them, and re-layouts: 8.81 us -> none
    pallas_call x1, Pallas kernels: 70.7 us -> 68.3 us  [local(): pl.pallas_call(functools.partial(exchange_kernel, cfg), out_shape=(jax.Sh...]
where the time goes in v2:
time: 73.2 us; the launch traced here: 72.9 us
  Pallas kernels  72.3 us (99%)
    pallas_call x1, Pallas kernels, local(): pl.pallas_call(functools.partial(exchange_kernel, cfg), out_shape=(jax.Sh...  68.3 us
    pallas_call x1, Pallas kernels, local(): pl.pallas_call(functools.partial(spread_kernel, (groups, cap, segs, resid...  3.94 us

profile of v2, /device:TPU:0, one launch (start us, length us, event | category | flops | bytes accessed | tf_op | source)
XLA Modules:
  0.0 72.9 jit_solution(15390940678116633975)
XLA Ops:
  0.6 68.3 %exchange.1 = (bf16[4,128,512]{2,1,0:T(8,128)(2,1)}, bf16[4,16,1024]{2,1,0:T(8,128)(2,1)}) custom-call(s32[4,4]{1,0:T(4,128)} %sai.3, s32[4,4]{1,0:T(4,128)} %cnt.1, s32[64]{0:T(128)} %row.3, bf16[128,4096]{1,0:T(8,128)(2,1)} %x.1, bf16[128,4096]{1,0:T(8,128)(2,1)} %q.1, bf16[128,1024]{1,0:T(8,128)(2,1)} %k.1, bf16[128,4096]{1,0:T(8,128)(2,1)} %o.1, ...), custom_call_target="tpu_custom_call" | custom-call | tf_op jit(solution)/shard_map/exchange/pallas_call | solution.py:436
  69.0 3.9 %spread.1 = (f32[16,64,512]{2,1,0:T(8,128)}, f32[16,8,1024]{2,1,0:T(8,128)}) custom-call(s32[4,4]{1,0:T(4,128)} %sai.3, s32[64]{0:T(128)} %row.3, bf16[512,512]{1,0:T(8,128)(2,1)} %bitcast.2, bf16[64,1024]{1,0:T(8,128)(2,1)} %bitcast.3), custom_call_target="tpu_custom_call" | custom-call | tf_op jit(solution)/shard_map/spread/pallas_call | solution.py:484
